TPU v7x, 32 devices: a whole 2x2x4 slice. The times are simulated.
32 devices in a mesh: depth: 4 (over z), plane: 8 (over y, x, core).
Axes of the slice: x: 2, y: 2, z: 4, core: 2. Of those that a mesh axis runs over, the one named last changes fastest.
Arguments:
- toar: bfloat16 [4, 8, 2, 16384], P('depth', None, None, 'plane'), may hold values from -6 to 6
- pml_coeff: float32 [4, 2, 16384], P('depth', None, 'plane'), may hold values from -1.5 to 1.5
- coupling: float32 [4, 16384], P('depth', 'plane'), may hold values from 0.5 to 1
- inverse: bfloat16 [4, 256, 16, 64, 128], P('depth', 'plane'), may hold values from -0.125 to 0.125
- pattern: int32 [4, 256, 16], P('depth', 'plane'), may hold values from 0 to 255
- patch_map: int32 [4, 16384], P('depth', 'plane'), may hold values from 0 to 4095, as said below
Outputs:
- precond: bfloat16 [4, 8, 2, 16384], P('depth', None, None, 'plane')
- patch_sens: float32 [8, 4096], P(None, ('depth', 'plane'))
Inputs may be any that keep to these rules, and one draw needn't show every extreme that they name: `patch_map`: patch p belongs to owner p // 128. Among the cells of one device (one layer, one block of 2048 cells), at most 128 name patches of any one owner, and in every such block some owner is named exactly 128 times. `pattern`: block columns of the whole layer.
All inputs are finite; a program needn't handle non-finite values.
Results may differ from a plain program's by a relative error of at most 0.018.
Values may be sent and summed in bfloat16 or wider, within the bound.
A program may use at most 128 MiB of HBM per device.

v0:
```python
import jax
import jax.numpy as jnp
from jax import lax
from jax.sharding import PartitionSpec as P

PATCH_DEV = 128


def passed_along(value, axis, steps):
    count = lax.axis_size(axis)
    first, last = (max(0, -steps), min(count, count - steps))
    return lax.ppermute(value, axis, [(source, source + steps) for source in range(first, last)])


def shards(toar, pml_coeff, coupling, inverse, pattern, patch_map):
    toar_local = toar[0]
    coeff = pml_coeff[0]
    coupler = coupling[0]
    inv_local = inverse[0]
    pattern_flat = pattern[0].reshape(-1)
    block_rows = inv_local.shape[0]
    per_row = inv_local.shape[1]
    block_cells = inv_local.shape[2]
    depth_count = lax.axis_size("depth")
    factor = inv_local.reshape(block_rows, per_row, block_cells, 2, block_cells)
    toar_f32 = toar_local.astype(jnp.float32)
    real_part = coeff[0] * toar_f32[:, 0] - coeff[1] * toar_f32[:, 1]
    imag_part = coeff[0] * toar_f32[:, 1] + coeff[1] * toar_f32[:, 0]
    source = jnp.stack([real_part, imag_part], axis=1)

    def apply_layer(incoming):
        gathered = lax.all_gather(incoming, "plane", axis=2, tiled=True)
        rows_here = gathered.shape[0]
        blocks = gathered.reshape(rows_here, 2, -1, block_cells)
        chosen = jnp.take(blocks, pattern_flat, axis=2)
        chosen = chosen.reshape(rows_here, 2, block_rows, per_row, block_cells)
        partial_value = jnp.einsum(
            "rkiaj,vbrkj->vabri", factor, chosen, preferred_element_type=jnp.float32
        )
        real_out = partial_value[:, 0, 0] - partial_value[:, 1, 1]
        imag_out = partial_value[:, 0, 1] + partial_value[:, 1, 0]
        return jnp.stack([real_out, imag_out], axis=1).reshape(
            rows_here, 2, block_rows * block_cells
        )

    def down_turn(turn_index, current):
        arrived = passed_along(current, "depth", 1)
        down_in = (source + coupler * arrived.astype(jnp.float32)).astype(jnp.bfloat16)
        return apply_layer(down_in).astype(jnp.bfloat16)

    first = apply_layer(source.astype(jnp.bfloat16)).astype(jnp.bfloat16)
    swept = lax.fori_loop(0, depth_count - 1, down_turn, first)

    def up_turn(turn_index, current):
        outgoing = (coupler * current.astype(jnp.float32)).astype(jnp.bfloat16)
        arrived = passed_along(outgoing, "depth", -1)
        return (swept.astype(jnp.float32) + apply_layer(arrived)).astype(jnp.bfloat16)

    precond = lax.fori_loop(0, depth_count - 1, up_turn, swept)
    product = precond.astype(jnp.float32) * toar_f32
    contrib = product[:, 0] + product[:, 1]
    cell_patch = patch_map[0]
    owner_count = depth_count * lax.axis_size("plane")
    patch_total = PATCH_DEV * owner_count
    local_sums = jax.ops.segment_sum(contrib.T, cell_patch, num_segments=patch_total).T
    owned = lax.psum_scatter(local_sums, ("depth", "plane"), scatter_dimension=1, tiled=True)
    return (precond[None], owned)


def solution(mesh):
    return jax.shard_map(
        shards,
        mesh=mesh,
        in_specs=(
            P("depth", None, None, "plane"),
            P("depth", None, "plane"),
            P("depth", "plane"),
            P("depth", "plane", None, None, None),
            P("depth", "plane", None),
            P("depth", "plane"),
        ),
        out_specs=(P("depth", None, None, "plane"), P(None, ("depth", "plane"))),
        check_vma=False,
    )
```

profile of v0, /device:TPU:0, one launch (start us, length us, event | category | flops | bytes accessed | tf_op | source)
XLA Modules:
  0.0 443.4 jit_solution(7410095448172458141)
XLA Ops:
  9.8 11.3 %all_gather.9 = bf16[8,2,16384]{2,0,1:T(8,128)(2,1)S(1)} all-gather(bf16[8,2,2048]{2,0,1:T(8,128)(2,1)S(1)} %fusion.32), channel_id=1, replica_groups=mesh['depth'=4,'plane'=8] {'plane'}, dimensions={2}, use_global_device_ids=true | all-gather | bytes 589824 | tf_op jit(solution)/shard_map/all_gather | solution.py:32
  23.0 27.8 %reshape_squeeze.7 = bf16[32,16,64,2,64]{4,3,2,1,0:T(2,128)(2,1)} reshape(bf16[1,32,16,64,128]{4,3,2,1,0:T(8,128)(2,1)} %param.15) | data formatting | bytes 16777216 | tf_op jit(solution)/shard_map/reshape;squeeze | solution.py:25
  50.8 15.2 %copy.28 = bf16[32,16,64,2,64]{4,2,1,3,0:T(8,128)(2,1)} copy(bf16[32,16,64,2,64]{4,3,2,1,0:T(2,128)(2,1)} %reshape_squeeze.7) | data formatting | bytes 16777216 | tf_op jit(solution)/shard_map/while | solution.py:52
  70.7 13.0 %fusion.22 = f32[8,2,2,32,64]{4,0,1,2,3:T(8,128)S(1)} fusion(bf16[32,16,64,2,64,1]{4,3,2,1,0,5:T(2,128)(2,1)} %bitcast.113, bf16[8,2,32,16,64,1]{4,0,1,3,2,5:T(8,128)(2,1)} %bitcast.115), kind=kOutput, calls=%fused_computation.35 | convolution fusion | flops 134217728 | bytes 9699328 | tf_op jit(solution)/shard_map/rkiaj,vbrkj->vabri/dot_general | solution.py:37
  84.1 100.4 %while.20 = (s32[]{:T(128)}, bf16[8,2,2048]{2,0,1:T(8,128)(2,1)S(1)}, f32[1,2048]{1,0:T(1,128)S(1)}, f32[8,2,2048]{2,0,1:T(8,128)S(1)}, s32[512]{0:T(512)S(1)}, /*index=5*/bf16[32,16,64,2,64]{4,2,1,3,0:T(8,128)(2,1)}, s32[]{:T(128)}) while((s32[]{:T(128)}, bf16[8,2,2048]{2,0,1:T(8,128)(2,1)S(1)}, f32[1,2048]{1,0:T(1,128)S(1)}, ...), condition=%wide.region_1.3_spmd, body=%wide.region_0.0_spmd.sunk | while | flops 134977024 | bytes 17849460 | solution.py:52
  84.3 3.5 collective-permute-start
  89.7 9.8 %all_gather.12 = bf16[8,2,16384]{2,0,1:T(8,128)(2,1)S(1)} all-gather(bf16[8,2,2048]{2,0,1:T(8,128)(2,1)S(1)} %add_convert_fusion.2), channel_id=1, replica_groups=mesh['depth'=4,'plane'=8] {'plane'}, dimensions={2}, use_global_device_ids=true | all-gather | bytes 589824 | tf_op jit(solution)/shard_map/while/body/eval_jaxpr/all_gather | solution.py:32
  104.1 2.9 broadcast_select_fusion.5
  107.0 10.1 %fusion.44 = f32[8,2,2,32,64]{4,0,1,2,3:T(8,128)S(1)} fusion(bf16[32,16,64,2,64]{4,2,1,3,0:T(8,128)(2,1)} %get-tuple-element.220, bf16[8,2,32,16,64,1]{4,0,1,3,2,5:T(8,128)(2,1)S(1)} %bitcast.111), kind=kOutput, calls=%fused_computation.8.clone.1 | convolution fusion | flops 134217728 | bytes 9699328 | tf_op jit(solution)/shard_map/while/body/eval_jaxpr/rkiaj,vbrkj->vabri/dot_general | solution.py:37
  117.4 4.4 collective-permute-start
  123.7 8.9 %all_gather.12 = bf16[8,2,16384]{2,0,1:T(8,128)(2,1)S(1)} all-gather(bf16[8,2,2048]{2,0,1:T(8,128)(2,1)S(1)} %add_convert_fusion.2), channel_id=1, replica_groups=mesh['depth'=4,'plane'=8] {'plane'}, dimensions={2}, use_global_device_ids=true | all-gather | bytes 589824 | tf_op jit(solution)/shard_map/while/body/eval_jaxpr/all_gather | solution.py:32
  137.1 2.9 broadcast_select_fusion.5
  140.0 10.1 %fusion.44 = f32[8,2,2,32,64]{4,0,1,2,3:T(8,128)S(1)} fusion(bf16[32,16,64,2,64]{4,2,1,3,0:T(8,128)(2,1)} %get-tuple-element.220, bf16[8,2,32,16,64,1]{4,0,1,3,2,5:T(8,128)(2,1)S(1)} %bitcast.111), kind=kOutput, calls=%fused_computation.8.clone.1 | convolution fusion | flops 134217728 | bytes 9699328 | tf_op jit(solution)/shard_map/while/body/eval_jaxpr/rkiaj,vbrkj->vabri/dot_general | solution.py:37
  150.5 4.4 collective-permute-start
  156.8 9.8 %all_gather.12 = bf16[8,2,16384]{2,0,1:T(8,128)(2,1)S(1)} all-gather(bf16[8,2,2048]{2,0,1:T(8,128)(2,1)S(1)} %add_convert_fusion.2), channel_id=1, replica_groups=mesh['depth'=4,'plane'=8] {'plane'}, dimensions={2}, use_global_device_ids=true | all-gather | bytes 589824 | tf_op jit(solution)/shard_map/while/body/eval_jaxpr/all_gather | solution.py:32
  171.2 2.9 broadcast_select_fusion.5
  174.1 10.1 %fusion.44 = f32[8,2,2,32,64]{4,0,1,2,3:T(8,128)S(1)} fusion(bf16[32,16,64,2,64]{4,2,1,3,0:T(8,128)(2,1)} %get-tuple-element.220, bf16[8,2,32,16,64,1]{4,0,1,3,2,5:T(8,128)(2,1)S(1)} %bitcast.111), kind=kOutput, calls=%fused_computation.8.clone.1 | convolution fusion | flops 134217728 | bytes 9699328 | tf_op jit(solution)/shard_map/while/body/eval_jaxpr/rkiaj,vbrkj->vabri/dot_general | solution.py:37
  184.5 100.7 %while.21 = (s32[]{:T(128)}, bf16[8,2,2048]{2,0,1:T(8,128)(2,1)S(1)}, bf16[8,2,2048]{2,0,1:T(8,128)(2,1)S(1)}, f32[1,2048]{1,0:T(1,128)S(1)}, s32[512]{0:T(512)S...) while((s32[]{:T(128)}, bf16[8,2,2048]{2,0,1:T(8,128)(2,1)S(1)}, bf16[8,2,2048]{2,0,1:T(8,128)(2,1)S(1)}, ...), condition=%wide.region_3.5_spmd, body=%wide.region_2.4_spmd.sunk | while | flops 135009792 | bytes 18177140 | solution.py:59
  185.9 5.6 %collective-permute-done.1 = bf16[8,2,2048]{2,0,1:T(8,128)(2,1)S(1)} collective-permute-done((bf16[8,2,2048]{2,0,1:T(8,128)(2,1)S(1)}, bf16[8,2,2048]{2,0,1:T(8,128)(2,1)S(1)}, u32[]{:S(2)}, u32[]{:S(2)}) %collective-permute-start.1) | collective-permute-done | bytes 65568 | tf_op jit(solution)/shard_map/while/body/eval_jaxpr/ppermute | solution.py:12
  191.5 8.9 %all_gather.13 = bf16[8,2,16384]{2,0,1:T(8,128)(2,1)S(1)} all-gather(bf16[8,2,2048]{2,0,1:T(8,128)(2,1)S(1)} %collective-permute-done.1), channel_id=1, replica_groups=mesh['depth'=4,'plane'=8] {'plane'}, dimensions={2}, use_global_device_ids=true | all-gather | bytes 589824 | tf_op jit(solution)/shard_map/while/body/eval_jaxpr/all_gather | solution.py:32
  205.0 2.9 broadcast_select_fusion.6
  207.9 10.1 %fusion.48 = f32[8,2,2,32,64]{4,0,1,2,3:T(8,128)S(1)} fusion(bf16[32,16,64,2,64]{4,2,1,3,0:T(8,128)(2,1)} %get-tuple-element.241, bf16[8,2,32,16,64,1]{4,0,1,3,2,5:T(8,128)(2,1)S(1)} %bitcast.112), kind=kOutput, calls=%fused_computation.22.clone.1 | convolution fusion | flops 134217728 | bytes 9699328 | tf_op jit(solution)/shard_map/while/body/eval_jaxpr/rkiaj,vbrkj->vabri/dot_general | solution.py:37
  219.7 4.9 %collective-permute-done.1 = bf16[8,2,2048]{2,0,1:T(8,128)(2,1)S(1)} collective-permute-done((bf16[8,2,2048]{2,0,1:T(8,128)(2,1)S(1)}, bf16[8,2,2048]{2,0,1:T(8,128)(2,1)S(1)}, u32[]{:S(2)}, u32[]{:S(2)}) %collective-permute-start.1) | collective-permute-done | bytes 65568 | tf_op jit(solution)/shard_map/while/body/eval_jaxpr/ppermute | solution.py:12
  224.6 9.8 %all_gather.13 = bf16[8,2,16384]{2,0,1:T(8,128)(2,1)S(1)} all-gather(bf16[8,2,2048]{2,0,1:T(8,128)(2,1)S(1)} %collective-permute-done.1), channel_id=1, replica_groups=mesh['depth'=4,'plane'=8] {'plane'}, dimensions={2}, use_global_device_ids=true | all-gather | bytes 589824 | tf_op jit(solution)/shard_map/while/body/eval_jaxpr/all_gather | solution.py:32
  238.9 2.9 broadcast_select_fusion.6
  241.8 10.1 %fusion.48 = f32[8,2,2,32,64]{4,0,1,2,3:T(8,128)S(1)} fusion(bf16[32,16,64,2,64]{4,2,1,3,0:T(8,128)(2,1)} %get-tuple-element.241, bf16[8,2,32,16,64,1]{4,0,1,3,2,5:T(8,128)(2,1)S(1)} %bitcast.112), kind=kOutput, calls=%fused_computation.22.clone.1 | convolution fusion | flops 134217728 | bytes 9699328 | tf_op jit(solution)/shard_map/while/body/eval_jaxpr/rkiaj,vbrkj->vabri/dot_general | solution.py:37
  253.6 4.9 %collective-permute-done.1 = bf16[8,2,2048]{2,0,1:T(8,128)(2,1)S(1)} collective-permute-done((bf16[8,2,2048]{2,0,1:T(8,128)(2,1)S(1)}, bf16[8,2,2048]{2,0,1:T(8,128)(2,1)S(1)}, u32[]{:S(2)}, u32[]{:S(2)}) %collective-permute-start.1) | collective-permute-done | bytes 65568 | tf_op jit(solution)/shard_map/while/body/eval_jaxpr/ppermute | solution.py:12
  258.5 8.9 %all_gather.13 = bf16[8,2,16384]{2,0,1:T(8,128)(2,1)S(1)} all-gather(bf16[8,2,2048]{2,0,1:T(8,128)(2,1)S(1)} %collective-permute-done.1), channel_id=1, replica_groups=mesh['depth'=4,'plane'=8] {'plane'}, dimensions={2}, use_global_device_ids=true | all-gather | bytes 589824 | tf_op jit(solution)/shard_map/while/body/eval_jaxpr/all_gather | solution.py:32
  272.0 2.9 broadcast_select_fusion.6
  274.9 10.1 %fusion.48 = f32[8,2,2,32,64]{4,0,1,2,3:T(8,128)S(1)} fusion(bf16[32,16,64,2,64]{4,2,1,3,0:T(8,128)(2,1)} %get-tuple-element.241, bf16[8,2,32,16,64,1]{4,0,1,3,2,5:T(8,128)(2,1)S(1)} %bitcast.112), kind=kOutput, calls=%fused_computation.22.clone.1 | convolution fusion | flops 134217728 | bytes 9699328 | tf_op jit(solution)/shard_map/while/body/eval_jaxpr/rkiaj,vbrkj->vabri/dot_general | solution.py:37
  285.7 13.0 %scatter_custom_fusion = f32[4096,8]{1,0:T(8,128)} fusion(s32[2048]{0:T(1024)} %bitcast.121, f32[2048,8]{1,0:T(8,128)S(1)} %copy.31, f32[]{:T(128)} %constant.3.clone.1), kind=kCustom, calls=%fused_computation.36 | custom fusion | flops 16384 | bytes 131584 | tf_op jit(solution)/shard_map/scatter-add | solution.py:65
  299.4 135.6 %reduce-scatter.2.cloned.1.call-done = f32[8,128]{0,1:T(8,128)} async-done(((f32[8,4096]{0,1:T(8,128)}), f32[8,128]{0,1:T(8,128)}) %reduce-scatter.2.cloned.1.call-update) | async-done | bytes 4112 | tf_op jit(solution)/shard_map/reduce_scatter | solution.py:66
  (116 shorter events, 51.1 us)
Async XLA Ops:
  7.2 427.9 %reduce-scatter.2.cloned.1.call-start = ((), (), s32[]{:S(2)}) async-start(), calls=%async_computation.1 | async-start | bytes 2162688 | tf_op jit(solution)/shard_map/reduce_scatter | solution.py:66
  70.7 13.4 %copy-start = (f32[1,2048]{1,0:T(1,128)S(1)}, f32[1,2048]{1,0:T(1,128)}, u32[]{:S(2)}) copy-start(f32[1,2048]{1,0:T(1,128)} %param.14) | copy-start | bytes 24580
  84.3 5.4 %collective-permute-start = (bf16[8,2,2048]{2,0,1:T(8,128)(2,1)S(1)}, bf16[8,2,2048]{2,0,1:T(8,128)(2,1)S(1)}, u32[]{:S(2)}, u32[]{:S(2)}) collective-permute-start(bf16[8,2,2048]{2,0,1:T(8,128)(2,1)S(1)} %get-tuple-element.209), channel_id=1, source_target_pairs={{0,8},{8,16},{16,24},{1,9},{9,17},{17,25},{2,10},{10,18},{18,26},{... | collective-permute-start | bytes 196616 | tf_op jit(solution)/shard_map/while/body/eval_jaxpr/ppermute | solution.py:12
  117.4 6.2 %collective-permute-start = (bf16[8,2,2048]{2,0,1:T(8,128)(2,1)S(1)}, bf16[8,2,2048]{2,0,1:T(8,128)(2,1)S(1)}, u32[]{:S(2)}, u32[]{:S(2)}) collective-permute-start(bf16[8,2,2048]{2,0,1:T(8,128)(2,1)S(1)} %get-tuple-element.209), channel_id=1, source_target_pairs={{0,8},{8,16},{16,24},{1,9},{9,17},{17,25},{2,10},{10,18},{18,26},{... | collective-permute-start | bytes 196616 | tf_op jit(solution)/shard_map/while/body/eval_jaxpr/ppermute | solution.py:12
  150.5 6.2 %collective-permute-start = (bf16[8,2,2048]{2,0,1:T(8,128)(2,1)S(1)}, bf16[8,2,2048]{2,0,1:T(8,128)(2,1)S(1)}, u32[]{:S(2)}, u32[]{:S(2)}) collective-permute-start(bf16[8,2,2048]{2,0,1:T(8,128)(2,1)S(1)} %get-tuple-element.209), channel_id=1, source_target_pairs={{0,8},{8,16},{16,24},{1,9},{9,17},{17,25},{2,10},{10,18},{18,26},{... | collective-permute-start | bytes 196616 | tf_op jit(solution)/shard_map/while/body/eval_jaxpr/ppermute | solution.py:12
  184.5 100.7 %copy-start.1 = (bf16[1,8,2,2048]{3,2,1,0:T(2,128)(2,1)S(1)}, bf16[1,8,2,2048]{3,2,1,0:T(2,128)(2,1)}, u32[]{:S(2)}) copy-start(bf16[1,8,2,2048]{3,2,1,0:T(2,128)(2,1)} %param.12) | copy-start | bytes 196612
  184.6 7.0 %collective-permute-start.1 = (bf16[8,2,2048]{2,0,1:T(8,128)(2,1)S(1)}, bf16[8,2,2048]{2,0,1:T(8,128)(2,1)S(1)}, u32[]{:S(2)}, u32[]{:S(2)}) collective-permute-start(bf16[8,2,2048]{2,0,1:T(8,128)(2,1)S(1)} %multiply_convert_fusion.2), channel_id=1, source_target_pairs={{8,0},{16,8},{24,16},{9,1},{17,9},{25,17},{10,2},{18,10},{26,18},{... | collective-permute-start | bytes 196616 | tf_op jit(solution)/shard_map/while/body/eval_jaxpr/ppermute | solution.py:12
  218.3 6.2 %collective-permute-start.1 = (bf16[8,2,2048]{2,0,1:T(8,128)(2,1)S(1)}, bf16[8,2,2048]{2,0,1:T(8,128)(2,1)S(1)}, u32[]{:S(2)}, u32[]{:S(2)}) collective-permute-start(bf16[8,2,2048]{2,0,1:T(8,128)(2,1)S(1)} %multiply_convert_fusion.2), channel_id=1, source_target_pairs={{8,0},{16,8},{24,16},{9,1},{17,9},{25,17},{10,2},{18,10},{26,18},{... | collective-permute-start | bytes 196616 | tf_op jit(solution)/shard_map/while/body/eval_jaxpr/ppermute | solution.py:12
  252.3 6.2 %collective-permute-start.1 = (bf16[8,2,2048]{2,0,1:T(8,128)(2,1)S(1)}, bf16[8,2,2048]{2,0,1:T(8,128)(2,1)S(1)}, u32[]{:S(2)}, u32[]{:S(2)}) collective-permute-start(bf16[8,2,2048]{2,0,1:T(8,128)(2,1)S(1)} %multiply_convert_fusion.2), channel_id=1, source_target_pairs={{8,0},{16,8},{24,16},{9,1},{17,9},{25,17},{10,2},{18,10},{26,18},{... | collective-permute-start | bytes 196616 | tf_op jit(solution)/shard_map/while/body/eval_jaxpr/ppermute | solution.py:12
Sparse Core Ops, SparseCore 0:
  298.8 136.1 reduce-scatter.1
where the time goes:
time: 445 us; the launch traced here: 443 us
  waiting for transfers between devices  157 us (35%)
  local copies, waits for them, and re-layouts  80.2 us (18%)
  matrix products  73.4 us (16%)
  blocking collectives  67.4 us (15%)
  other arithmetic  34.6 us (8%)
  starting transfers between devices  16.1 us (4%)
  between operations  14.2 us (3%)
    reduce_scatter x1, waiting for transfers between devices, shards(): lax.psum_scatter(local_sums, ('depth', 'plane'), scatter_dimension=1, til...  136 us
    dot_general x7, matrix products, apply_layer(): jnp.einsum('rkiaj,vbrkj->vabri', factor, chosen, preferred_element_type=j...  73.4 us
    all_gather x7, blocking collectives, apply_layer(): gathered = lax.all_gather(incoming, 'plane', axis=2, tiled=True)  67.4 us
    another operation x1, local copies, waits for them, and re-layouts, shards(): factor = inv_local.reshape(block_rows, per_row, block_cells, 2, block_cells)  27.8 us
    ppermute x6, waiting for transfers between devices, passed_along(): lax.ppermute(value, axis, [(source, source + steps) for source in range(f...  21 us
    select_n x14, other arithmetic, apply_layer(): chosen = jnp.take(blocks, pattern_flat, axis=2)  20 us
    gather x7, local copies, waits for them, and re-layouts, apply_layer(): chosen = jnp.take(blocks, pattern_flat, axis=2)  18.5 us
    ppermute x6, starting transfers between devices, passed_along(): lax.ppermute(value, axis, [(source, source + steps) for source in range(f...  16.1 us
  transfers between devices with their start and end apart: 7, of which 7 were waited for; matrix products, arithmetic and copies ran while one was open for 0% of the time, Pallas kernels for 0%

commit v1 on v0

v1 whole, which is shorter than its diff:
```python
import functools

import jax
import jax.numpy as jnp
from jax import lax
from jax.experimental import pallas as pl
from jax.experimental.pallas import tpu as pltpu
from jax.sharding import PartitionSpec as P

PATCH_DEV = 128
CHUNKS = 4
F32 = jnp.float32
BF16 = jnp.bfloat16


def sweep_kernel(
    depths, planes, pairs, chunks, per_row, vecs,
    pat, src, coup, toar, owner, slot, inv_hbm,
    pre, owned,
    inv, xg, xp, zdn, swept, up, lhs, onehot, part, r1, s1, r2,
    isem, gs, gr, zs, zr, us, ur, as_, ar, bs, br,
):
    d = lax.axis_index("depth")
    p = lax.axis_index("plane")
    step = pairs // chunks
    rows = 2 * step
    owners = depths * planes

    def load(c):
        part_rows = pl.ds(c * rows, rows)
        return pltpu.make_async_copy(inv_hbm.at[part_rows], inv.at[part_rows], isem.at[c])

    for c in range(chunks):
        load(c).start()

    barrier = pltpu.get_barrier_semaphore()

    def greet_plane(o, _):
        pl.semaphore_signal(barrier, inc=1, device_id=(d, lax.rem(p + o, planes)),
                            device_id_type=pl.DeviceIdType.MESH)
        return 0

    def greet_depth(o, _):
        pl.semaphore_signal(barrier, inc=1, device_id=(lax.rem(d + o, depths), p),
                            device_id_type=pl.DeviceIdType.MESH)
        return 0

    lax.fori_loop(1, planes, greet_plane, 0)
    lax.fori_loop(1, depths, greet_depth, 0)
    pl.semaphore_wait(barrier, planes + depths - 2)

    def remote(src_ref, dst_ref, send, recv, target):
        return pltpu.make_async_remote_copy(
            src_ref=src_ref, dst_ref=dst_ref, send_sem=send, recv_sem=recv,
            device_id=target, device_id_type=pl.DeviceIdType.MESH)

    def cut(q, c):
        return pl.ds(q * pairs + c * step, step)

    def gather_copy(phase, o, c, q, target):
        block = xg.at[phase, cut(q, c)]
        return remote(block, block, gs.at[phase, o - 1, c], gr.at[phase, o - 1, c], (d, target))

    def down_copy(c):
        here = pl.ds(c * step, step)
        return remote(swept.at[here], zdn.at[here], zs.at[c], zr.at[c], (lax.rem(d + 1, depths), p))

    def up_copy(c):
        return remote(up.at[pl.ds(c * step, step)], xg.at[1, cut(p, c)], us.at[c], ur.at[c],
                      (lax.rem(d + depths - 1, depths), p))

    left = lax.broadcasted_iota(jnp.int32, (vecs, 128), 1) < 64

    def expand(phase, q):
        def one(i, _):
            n = q * pairs + i
            both = xg[phase, n].astype(F32)
            re, im = both[:vecs], both[vecs:]
            re_t, im_t = pltpu.roll(re, 64, 1), pltpu.roll(im, 64, 1)
            xp[2 * n] = jnp.concatenate(
                [jnp.where(left, re, -im_t), jnp.where(left, im, re_t)], 0).astype(BF16)
            xp[2 * n + 1] = jnp.concatenate(
                [jnp.where(left, re_t, -im), jnp.where(left, im_t, re)], 0).astype(BF16)
            return 0

        lax.fori_loop(0, pairs, one, 0, unroll=4)

    def push(phase, c):
        def one(o, _):
            gather_copy(phase, o, c, p, lax.rem(p + o, planes)).start()
            return 0

        lax.fori_loop(1, planes, one, 0)

    def collect(phase):
        expand(phase, p)

        def one(o, _):
            q = lax.rem(p + planes - o, planes)
            for c in range(chunks):
                gather_copy(phase, o, c, q, q).wait_recv()
            expand(phase, q)
            return 0

        lax.fori_loop(1, planes, one, 0)

    def sent(phase):
        def one(o, _):
            for c in range(chunks):
                gather_copy(phase, o, c, p, lax.rem(p + o, planes)).wait_send()
            return 0

        lax.fori_loop(1, planes, one, 0)

    def block_row(r):
        x = jnp.concatenate([xp[pat[r * per_row + k]] for k in range(per_row)], 1)
        w = jnp.concatenate([inv[r, k] for k in range(per_row)], 1)
        return lax.dot_general(x, w, (((1,), (1,)), ((), ())), preferred_element_type=F32)

    def product(i):
        return jnp.concatenate([block_row(2 * i), block_row(2 * i + 1)], 1)

    def send_up(c):
        @pl.when(d > 0)
        def _():
            def one(i, _):
                n = c * step + i
                up[n] = (coup[n] * pre[n].astype(F32)).astype(BF16)
                return 0

            lax.fori_loop(0, step, one, 0)
            up_copy(c).start()

    @pl.when(d == 0)
    def _():
        zdn[...] = jnp.zeros_like(zdn)

    for c in range(chunks):
        @pl.when(d > 0)
        def _():
            down_copy(c).wait_recv()

        def one(i, _):
            n = c * step + i
            xg[0, p * pairs + n] = (src[n] + coup[n] * zdn[n].astype(F32)).astype(BF16)
            return 0

        lax.fori_loop(0, step, one, 0, unroll=True)
        push(0, c)

    lanes = lax.broadcasted_iota(jnp.int32, (PATCH_DEV, onehot.shape[1]), 0)
    onehot[...] = jnp.where(lanes == slot[...], 1.0, 0.0).astype(BF16)

    collect(0)

    def down_chunk(c, _):
        load(c).wait()

        def one(i, _):
            n = c * step + i
            swept[n] = product(n).astype(BF16)
            return 0

        lax.fori_loop(0, step, one, 0)

        @pl.when(d < depths - 1)
        def _():
            down_copy(c).start()

        @pl.when(d == depths - 1)
        def _():
            def keep(i, _):
                pre[c * step + i] = swept[c * step + i]
                return 0

            lax.fori_loop(0, step, keep, 0)
            send_up(c)

        return 0

    lax.fori_loop(0, chunks, down_chunk, 0)

    @pl.when(d < depths - 1)
    def _():
        for c in range(chunks):
            up_copy(c).wait_recv()
            push(1, c)
        collect(1)

        def up_chunk(c, _):
            def one(i, _):
                n = c * step + i
                pre[n] = (swept[n].astype(F32) + product(n)).astype(BF16)
                return 0

            lax.fori_loop(0, step, one, 0)
            send_up(c)
            return 0

        lax.fori_loop(0, chunks, up_chunk, 0)

    terms = []
    for i in range(pairs):
        both = pre[i].astype(F32) * toar[i].astype(F32)
        terms.append(both[:vecs] + both[vecs:])
    contrib = jnp.concatenate(terms, 1)
    named = jnp.broadcast_to(owner[...], contrib.shape)

    def mask(h, _):
        lhs[h] = jnp.concatenate(
            [jnp.where(named == 2 * h, contrib, 0.0), jnp.where(named == 2 * h + 1, contrib, 0.0)],
            0).astype(BF16)
        return 0

    lax.fori_loop(0, owners // 2, mask, 0)
    part[...] = lax.dot_general(
        lhs[...].reshape(owners * vecs, lhs.shape[2]), onehot[...], (((1,), (1,)), ((), ())),
        preferred_element_type=F32).reshape(owners, vecs, PATCH_DEV)

    def first(o):
        t = lax.rem(d + o, depths)
        return remote(part.at[pl.ds(t * planes, planes)], r1.at[o - 1], as_.at[o - 1], ar.at[o - 1], (t, p))

    for o in range(1, depths):
        first(o).start()
    total = part[pl.ds(d * planes, planes)]
    for o in range(1, depths):
        first(o).wait_recv()
        total = total + r1[o - 1]
    s1[...] = total

    def second(o):
        t = lax.rem(p + o, planes)
        return remote(s1.at[t], r2.at[o - 1], bs.at[o - 1], br.at[o - 1], (d, t))

    for o in range(1, planes):
        second(o).start()
    last = s1[p]
    for o in range(1, planes):
        second(o).wait_recv()
        last = last + r2[o - 1]
    owned[...] = last

    sent(0)

    @pl.when(d < depths - 1)
    def _():
        sent(1)
        for c in range(chunks):
            down_copy(c).wait_send()

    @pl.when(d > 0)
    def _():
        for c in range(chunks):
            up_copy(c).wait_send()

    for o in range(1, depths):
        first(o).wait_send()
    for o in range(1, planes):
        second(o).wait_send()


def shards(toar, pml_coeff, coupling, inverse, pattern, patch_map):
    depths, planes = lax.axis_size("depth"), lax.axis_size("plane")
    _, vecs, _, cells = toar.shape
    block_rows, per_row, blk = inverse.shape[1:4]
    pairs = cells // 128
    owners = depths * planes

    def tiles(value):
        return value.reshape(2 * vecs, pairs, 128).transpose(1, 0, 2)

    vectors = toar[0].transpose(1, 0, 2)
    wide = vectors.astype(F32)
    coeff = pml_coeff[0][:, None]
    source = jnp.concatenate(
        [coeff[0] * wide[0] - coeff[1] * wide[1], coeff[0] * wide[1] + coeff[1] * wide[0]], 0)
    patches = patch_map[0][None]
    tile = (pairs, 2 * vecs, 128)
    vmem = pl.BlockSpec(memory_space=pltpu.VMEM)
    dma = pltpu.SemaphoreType.DMA
    pre, owned = pl.pallas_call(
        functools.partial(sweep_kernel, depths, planes, pairs, CHUNKS, per_row, vecs),
        out_shape=(jax.ShapeDtypeStruct(tile, BF16), jax.ShapeDtypeStruct((vecs, PATCH_DEV), F32)),
        in_specs=[pl.BlockSpec(memory_space=pltpu.SMEM)] + [vmem] * 5 + [pl.BlockSpec(memory_space=pl.ANY)],
        out_specs=(vmem, vmem),
        scratch_shapes=[
            pltpu.VMEM((block_rows, per_row, blk, 2 * blk), BF16),
            pltpu.VMEM((2, planes * pairs, 2 * vecs, 128), BF16),
            pltpu.VMEM((planes * block_rows, 2 * vecs, 128), BF16),
            pltpu.VMEM(tile, BF16),
            pltpu.VMEM(tile, BF16),
            pltpu.VMEM(tile, BF16),
            pltpu.VMEM((owners // 2, 2 * vecs, cells), BF16),
            pltpu.VMEM((PATCH_DEV, cells), BF16),
            pltpu.VMEM((owners, vecs, PATCH_DEV), F32),
            pltpu.VMEM((depths - 1, planes, vecs, PATCH_DEV), F32),
            pltpu.VMEM((planes, vecs, PATCH_DEV), F32),
            pltpu.VMEM((planes - 1, vecs, PATCH_DEV), F32),
            dma((CHUNKS,)),
            dma((2, planes - 1, CHUNKS)),
            dma((2, planes - 1, CHUNKS)),
            dma((CHUNKS,)),
            dma((CHUNKS,)),
            dma((CHUNKS,)),
            dma((CHUNKS,)),
            dma((depths - 1,)),
            dma((depths - 1,)),
            dma((planes - 1,)),
            dma((planes - 1,)),
        ],
        compiler_params=pltpu.CompilerParams(
            collective_id=0, has_side_effects=True, vmem_limit_bytes=40 * 1024 * 1024),
        cost_estimate=pl.CostEstimate(
            flops=4 * block_rows * per_row * blk * 2 * blk * 2 * vecs,
            bytes_accessed=2 * block_rows * per_row * blk * 2 * blk, transcendentals=0),
    )(
        pattern[0].reshape(-1), tiles(source), coupling[0].reshape(pairs, 1, 128),
        tiles(vectors), patches // PATCH_DEV, patches % PATCH_DEV, inverse[0],
    )
    precond = pre.transpose(1, 0, 2).reshape(2, vecs, cells).transpose(1, 0, 2)
    return (precond[None], owned)


def solution(mesh):
    return jax.shard_map(
        shards,
        mesh=mesh,
        in_specs=(
            P("depth", None, None, "plane"),
            P("depth", None, "plane"),
            P("depth", "plane"),
            P("depth", "plane", None, None, None),
            P("depth", "plane", None),
            P("depth", "plane"),
        ),
        out_specs=(P("depth", None, None, "plane"), P(None, ("depth", "plane"))),
        check_vma=False,
    )
```

time: 445 us -> 118 us (0.27)
  the two profiles are of different devices: /device:TPU:0 before, /device:TPU:25 now
where the time goes in v1:
time: 118 us; the launch traced here: 117 us
  Pallas kernels  106 us (90%)
  local copies, waits for them, and re-layouts  8.09 us (7%)
  other arithmetic  2.41 us (2%)
    pallas_call x1, Pallas kernels, shards(): pl.pallas_call(functools.partial(sweep_kernel, depths, planes, pairs, CHU...  106 us
    unnamed x8, local copies, waits for them, and re-layouts  6.16 us

profile of v1, /device:TPU:25, one launch (start us, length us, event | category | flops | bytes accessed | tf_op | source)
XLA Modules:
  0.0 117.1 jit_solution(17328076093814419349)
XLA Ops:
  0.6 0.9 bitcast_convert_fusion
  1.5 0.1 fusion
  1.6 0.8 fusion.1
  2.4 0.1 multiply_subtract_fusion
  2.5 0.7 and_select_fusion
  3.3 0.7 and_select_fusion.1.owner
  4.0 0.9 copy.25
  4.9 0.8 copy.8
  5.7 0.1 reshape_squeeze.6.pat
  5.8 0.0 copy-start
  5.8 3.4 %copy-done = bf16[1,32,16,64,128]{4,3,2,1,0:T(8,128)(2,1)S(1)} copy-done((bf16[1,32,16,64,128]{4,3,2,1,0:T(8,128)(2,1)S(1)}, bf16[1,32,16,64,128]{4,3,2,1,0:T(8,128)(2,1)}, u32[]{:S(2)}) %copy-start) | copy-done | bytes 8388632
  9.1 0.0 copy-start.1
  9.1 0.7 copy-done.1
  9.8 105.9 %shard_map.77 = (bf16[16,16,128]{2,1,0:T(8,128)(2,1)S(1)}, f32[8,128]{1,0:T(8,128)S(1)}) custom-call(s32[512]{0:T(512)S(1)} %reshape_squeeze.6.pat, f32[16,16,128]{2,1,0:T(8,128)S(1)} %maximum_bitcast_fusion.src, f32[16,1,128]{2,1,0:T(1,128)S(1)} %bitcast.27, bf16[16,16,128]{2,1,0:T(8,128)(2,1)S(1)} %bitcast.25, s32[1,2048]{1,0:T(1,128)S(1)} %and_select_fusion.1.owner, ...), custom_call_target="tpu_custom_call" | custom-call | flops 268435456 | bytes 8388608 | tf_op jit(solution)/shard_map/pallas_call | solution.py:282
  115.8 0.7 copy.16
  116.5 0.6 copy.27
  (5 shorter events, 0.1 us)
Async XLA Ops:
  5.8 3.4 %copy-start = (bf16[1,32,16,64,128]{4,3,2,1,0:T(8,128)(2,1)S(1)}, bf16[1,32,16,64,128]{4,3,2,1,0:T(8,128)(2,1)}, u32[]{:S(2)}) copy-start(bf16[1,32,16,64,128]{4,3,2,1,0:T(8,128)(2,1)} %param.9) | copy-start | bytes 25165828
  9.1 0.7 copy-start.1

commit v2 on v1

--- a/solution.py
+++ b/solution.py
@@ -15,7 +15,7 @@
 
 def sweep_kernel(
     depths, planes, pairs, chunks, per_row, vecs,
-    pat, src, coup, toar, owner, slot, inv_hbm,
+    pat, src, coup, toar, patch, inv_hbm,
     pre, owned,
     inv, xg, xp, zdn, swept, up, lhs, onehot, part, r1, s1, r2,
     isem, gs, gr, zs, zr, us, ur, as_, ar, bs, br,
@@ -57,9 +57,27 @@
     def cut(q, c):
         return pl.ds(q * pairs + c * step, step)
 
-    def gather_copy(phase, o, c, q, target):
+    groups = planes // 2
+    group, twin = p // 2, p % 2
+    partner = 2 * group + 1 - twin
+
+    def twin_of(j):
+        return 2 * lax.rem(group + j, groups) + twin
+
+    def from_twin(j):
+        return 2 * lax.rem(group + groups - j, groups) + twin
+
+    def from_partner(j):
+        return 2 * lax.rem(group + groups - j, groups) + 1 - twin
+
+    def twin_copy(phase, j, c, q, target):
         block = xg.at[phase, cut(q, c)]
-        return remote(block, block, gs.at[phase, o - 1, c], gr.at[phase, o - 1, c], (d, target))
+        return remote(block, block, gs.at[phase, j - 1, c], gr.at[phase, j - 1, c], (d, target))
+
+    def partner_copy(phase, j, c, q):
+        block = xg.at[phase, cut(q, c)]
+        n = groups - 1 + j
+        return remote(block, block, gs.at[phase, n, c], gr.at[phase, n, c], (d, partner))
 
     def down_copy(c):
         here = pl.ds(c * step, step)
@@ -86,39 +104,64 @@
         lax.fori_loop(0, pairs, one, 0, unroll=4)
 
     def push(phase, c):
-        def one(o, _):
-            gather_copy(phase, o, c, p, lax.rem(p + o, planes)).start()
-            return 0
-
-        lax.fori_loop(1, planes, one, 0)
+        def one(j, _):
+            twin_copy(phase, j, c, p, twin_of(j)).start()
+            return 0
+
+        lax.fori_loop(1, groups, one, 0)
+        partner_copy(phase, 0, c, p).start()
 
     def collect(phase):
         expand(phase, p)
-
-        def one(o, _):
-            q = lax.rem(p + planes - o, planes)
+        for c in range(chunks):
+            def hand(j, _):
+                q = from_twin(j)
+                twin_copy(phase, j, c, q, q).wait_recv()
+                partner_copy(phase, j, c, q).start()
+                return 0
+
+            lax.fori_loop(1, groups, hand, 0)
+
+        def near(j, _):
+            expand(phase, from_twin(j))
+            return 0
+
+        lax.fori_loop(1, groups, near, 0)
+
+        def far(j, _):
+            q = from_partner(j)
             for c in range(chunks):
-                gather_copy(phase, o, c, q, q).wait_recv()
+                partner_copy(phase, j, c, q).wait_recv()
             expand(phase, q)
             return 0
 
-        lax.fori_loop(1, planes, one, 0)
+        lax.fori_loop(0, groups, far, 0)
 
     def sent(phase):
-        def one(o, _):
+        def one(j, _):
             for c in range(chunks):
-                gather_copy(phase, o, c, p, lax.rem(p + o, planes)).wait_send()
-            return 0
-
-        lax.fori_loop(1, planes, one, 0)
-
-    def block_row(r):
-        x = jnp.concatenate([xp[pat[r * per_row + k]] for k in range(per_row)], 1)
-        w = jnp.concatenate([inv[r, k] for k in range(per_row)], 1)
-        return lax.dot_general(x, w, (((1,), (1,)), ((), ())), preferred_element_type=F32)
+                twin_copy(phase, j, c, p, twin_of(j)).wait_send()
+            return 0
+
+        def other(j, _):
+            for c in range(chunks):
+                partner_copy(phase, j, c, from_twin(j)).wait_send()
+            return 0
+
+        lax.fori_loop(1, groups, one, 0)
+        lax.fori_loop(0, groups, other, 0)
+
+    left_all = lax.broadcasted_iota(jnp.int32, (2 * vecs, 128), 1) < 64
 
     def product(i):
-        return jnp.concatenate([block_row(2 * i), block_row(2 * i + 1)], 1)
+        x = jnp.concatenate(
+            [jnp.concatenate([xp[pat[(4 * i + m) * per_row + k]] for k in range(per_row)], 1)
+             for m in range(4)], 0)
+        w = jnp.concatenate([inv[pl.ds(4 * i, 4), k].reshape(256, 128) for k in range(per_row)], 1)
+        y = lax.dot_general(x, w, (((1,), (1,)), ((), ())), preferred_element_type=F32)
+        n = 2 * vecs
+        return (jnp.where(left_all, y[:n, :128], y[n:2 * n, :128]),
+                jnp.where(left_all, y[2 * n:3 * n, 128:], y[3 * n:, 128:]))
 
     def send_up(c):
         @pl.when(d > 0)
@@ -149,7 +192,7 @@
         push(0, c)
 
     lanes = lax.broadcasted_iota(jnp.int32, (PATCH_DEV, onehot.shape[1]), 0)
-    onehot[...] = jnp.where(lanes == slot[...], 1.0, 0.0).astype(BF16)
+    onehot[...] = jnp.where(lanes == patch[...] % PATCH_DEV, 1.0, 0.0).astype(BF16)
 
     collect(0)
 
@@ -157,11 +200,13 @@
         load(c).wait()
 
         def one(i, _):
-            n = c * step + i
-            swept[n] = product(n).astype(BF16)
-            return 0
-
-        lax.fori_loop(0, step, one, 0)
+            n = c * step + 2 * i
+            lower, upper = product(c * (step // 2) + i)
+            swept[n] = lower.astype(BF16)
+            swept[n + 1] = upper.astype(BF16)
+            return 0
+
+        lax.fori_loop(0, step // 2, one, 0)
 
         @pl.when(d < depths - 1)
         def _():
@@ -189,11 +234,13 @@
 
         def up_chunk(c, _):
             def one(i, _):
-                n = c * step + i
-                pre[n] = (swept[n].astype(F32) + product(n)).astype(BF16)
+                n = c * step + 2 * i
+                lower, upper = product(c * (step // 2) + i)
+                pre[n] = (swept[n].astype(F32) + lower).astype(BF16)
+                pre[n + 1] = (swept[n + 1].astype(F32) + upper).astype(BF16)
                 return 0
 
-            lax.fori_loop(0, step, one, 0)
+            lax.fori_loop(0, step // 2, one, 0)
             send_up(c)
             return 0
 
@@ -204,7 +251,7 @@
         both = pre[i].astype(F32) * toar[i].astype(F32)
         terms.append(both[:vecs] + both[vecs:])
     contrib = jnp.concatenate(terms, 1)
-    named = jnp.broadcast_to(owner[...], contrib.shape)
+    named = jnp.broadcast_to(patch[...] // PATCH_DEV, contrib.shape)
 
     def mask(h, _):
         lhs[h] = jnp.concatenate(
@@ -275,14 +322,13 @@
     coeff = pml_coeff[0][:, None]
     source = jnp.concatenate(
         [coeff[0] * wide[0] - coeff[1] * wide[1], coeff[0] * wide[1] + coeff[1] * wide[0]], 0)
-    patches = patch_map[0][None]
     tile = (pairs, 2 * vecs, 128)
     vmem = pl.BlockSpec(memory_space=pltpu.VMEM)
     dma = pltpu.SemaphoreType.DMA
     pre, owned = pl.pallas_call(
         functools.partial(sweep_kernel, depths, planes, pairs, CHUNKS, per_row, vecs),
         out_shape=(jax.ShapeDtypeStruct(tile, BF16), jax.ShapeDtypeStruct((vecs, PATCH_DEV), F32)),
-        in_specs=[pl.BlockSpec(memory_space=pltpu.SMEM)] + [vmem] * 5 + [pl.BlockSpec(memory_space=pl.ANY)],
+        in_specs=[pl.BlockSpec(memory_space=pltpu.SMEM)] + [vmem] * 4 + [pl.BlockSpec(memory_space=pl.ANY)],
         out_specs=(vmem, vmem),
         scratch_shapes=[
             pltpu.VMEM((block_rows, per_row, blk, 2 * blk), BF16),
@@ -310,13 +356,13 @@
             dma((planes - 1,)),
         ],
         compiler_params=pltpu.CompilerParams(
-            collective_id=0, has_side_effects=True, vmem_limit_bytes=40 * 1024 * 1024),
+            collective_id=0, has_side_effects=True, vmem_limit_bytes=56 * 1024 * 1024),
         cost_estimate=pl.CostEstimate(
             flops=4 * block_rows * per_row * blk * 2 * blk * 2 * vecs,
             bytes_accessed=2 * block_rows * per_row * blk * 2 * blk, transcendentals=0),
     )(
         pattern[0].reshape(-1), tiles(source), coupling[0].reshape(pairs, 1, 128),
-        tiles(vectors), patches // PATCH_DEV, patches % PATCH_DEV, inverse[0],
+        tiles(vectors), patch_map, inverse[0],
     )
     precond = pre.transpose(1, 0, 2).reshape(2, vecs, cells).transpose(1, 0, 2)
     return (precond[None], owned)

time: 118 us -> 105 us (0.89)
  Pallas kernels: 106 us -> 95.6 us
  local copies, waits for them, and re-layouts: 8.09 us -> 6.72 us
    pallas_call x1, Pallas kernels: 106 us -> 95.6 us  [shards(): pl.pallas_call(functools.partial(sweep_kernel, depths, planes, pairs, CHU...]
    unnamed x8 -> x4, local copies, waits for them, and re-layouts: 6.16 us -> 2.75 us
    select_n x2 -> x0, other arithmetic: 1.46 us -> none  [the longest x1 0.73 us: shards(): patches // PATCH_DEV]
where the time goes in v2:
time: 105 us
  Pallas kernels  95.6 us (91%)
  local copies, waits for them, and re-layouts  6.72 us (6%)
  other arithmetic  1.59 us (2%)
    pallas_call x1, Pallas kernels, shards(): pl.pallas_call(functools.partial(sweep_kernel, depths, planes, pairs, CHU...  95.6 us
    unnamed x4, local copies, waits for them, and re-layouts  2.75 us

profile of v2, /device:TPU:25, one launch (start us, length us, event | category | flops | bytes accessed | tf_op | source)
XLA Modules:
  0.0 104.6 jit_solution(569301052867603112)
XLA Ops:
  0.6 0.9 bitcast_convert_fusion
  1.5 0.1 fusion
  1.6 0.8 fusion.1
  2.4 0.1 multiply_subtract_fusion
  2.5 0.7 maximum_bitcast_fusion.src
  3.2 0.9 copy.25
  4.0 0.6 copy.24
  4.7 0.8 copy.8
  5.5 0.7 reshape_squeeze.6.pat
  6.1 95.6 %shard_map.77 = (bf16[16,16,128]{2,1,0:T(8,128)(2,1)}, f32[8,128]{1,0:T(8,128)}) custom-call(s32[512]{0:T(512)} %reshape_squeeze.6.pat, f32[16,16,128]{2,1,0:T(8,128)} %maximum_bitcast_fusion.src, f32[16,1,128]{2,1,0:T(1,128)} %bitcast.35, bf16[16,16,128]{2,1,0:T(8,128)(2,1)} %bitcast.25, s32[1,2048]{1,0:T(1,128)} %patch.1, bf16[32,16,64,128]{3,2,1,0:T(8,128)(2,1)} %bitcast.24), custom_call_target="tpu_custom_call" | custom-call | flops 268435456 | bytes 8388608 | tf_op jit(solution)/shard_map/pallas_call | solution.py:328
  101.7 0.9 copy.15
  102.6 0.7 copy.16
  103.3 1.3 %copy.27 = f32[8,128]{1,0:T(8,128)} copy(f32[8,128]{1,0:T(8,128)} %get-tuple-element.17) | data formatting | bytes 8192
  (2 shorter events, 0.0 us)

commit v3 on v2

--- a/solution.py
+++ b/solution.py
@@ -87,21 +87,19 @@
         return remote(up.at[pl.ds(c * step, step)], xg.at[1, cut(p, c)], us.at[c], ur.at[c],
                       (lax.rem(d + depths - 1, depths), p))
 
-    left = lax.broadcasted_iota(jnp.int32, (vecs, 128), 1) < 64
+    left = lax.broadcasted_iota(jnp.int32, (pairs // 2, vecs, 128), 2) < 64
 
     def expand(phase, q):
-        def one(i, _):
-            n = q * pairs + i
-            both = xg[phase, n].astype(F32)
-            re, im = both[:vecs], both[vecs:]
-            re_t, im_t = pltpu.roll(re, 64, 1), pltpu.roll(im, 64, 1)
-            xp[2 * n] = jnp.concatenate(
-                [jnp.where(left, re, -im_t), jnp.where(left, im, re_t)], 0).astype(BF16)
-            xp[2 * n + 1] = jnp.concatenate(
-                [jnp.where(left, re_t, -im), jnp.where(left, im_t, re)], 0).astype(BF16)
-            return 0
-
-        lax.fori_loop(0, pairs, one, 0, unroll=4)
+        half = pairs // 2
+        for h in range(2):
+            n = q * pairs + h * half
+            both = xg[phase, pl.ds(n, half)].astype(F32)
+            re, im = both[:, :vecs], both[:, vecs:]
+            re_t, im_t = pltpu.roll(re, 64, 2), pltpu.roll(im, 64, 2)
+            even = jnp.concatenate([jnp.where(left, re, -im_t), jnp.where(left, im, re_t)], 1)
+            odd = jnp.concatenate([jnp.where(left, re_t, -im), jnp.where(left, im_t, re)], 1)
+            tiles = jnp.stack([even, odd], 1).reshape(2 * half, 2 * vecs, 128)
+            xp[pl.ds(2 * n, 2 * half)] = tiles.astype(BF16)
 
     def push(phase, c):
         def one(j, _):

time: 105 us -> 96 us (0.914)
  Pallas kernels: 95.6 us -> 86.5 us
    pallas_call x1, Pallas kernels: 95.6 us -> 86.5 us  [shards(): pl.pallas_call(functools.partial(sweep_kernel, depths, planes, pairs, CHU...]
where the time goes in v3:
time: 96 us; the launch traced here: 95.5 us
  Pallas kernels  86.5 us (90%)
  local copies, waits for them, and re-layouts  6.72 us (7%)
  other arithmetic  1.59 us (2%)
    pallas_call x1, Pallas kernels, shards(): pl.pallas_call(functools.partial(sweep_kernel, depths, planes, pairs, CHU...  86.5 us
    unnamed x4, local copies, waits for them, and re-layouts  2.75 us

profile of v3, /device:TPU:25, one launch (start us, length us, event | category | flops | bytes accessed | tf_op | source)
XLA Modules:
  0.0 95.5 jit_solution(17564364157706775670)
XLA Ops:
  0.6 0.9 bitcast_convert_fusion
  1.5 0.1 fusion
  1.6 0.8 fusion.1
  2.4 0.1 multiply_subtract_fusion
  2.5 0.7 maximum_bitcast_fusion.src
  3.2 0.9 copy.25
  4.0 0.6 copy.24
  4.7 0.8 copy.8
  5.5 0.7 reshape_squeeze.6.pat
  6.1 86.5 %shard_map.77 = (bf16[16,16,128]{2,1,0:T(8,128)(2,1)}, f32[8,128]{1,0:T(8,128)}) custom-call(s32[512]{0:T(512)} %reshape_squeeze.6.pat, f32[16,16,128]{2,1,0:T(8,128)} %maximum_bitcast_fusion.src, f32[16,1,128]{2,1,0:T(1,128)} %bitcast.35, bf16[16,16,128]{2,1,0:T(8,128)(2,1)} %bitcast.25, s32[1,2048]{1,0:T(1,128)} %patch.1, bf16[32,16,64,128]{3,2,1,0:T(8,128)(2,1)} %bitcast.24), custom_call_target="tpu_custom_call" | custom-call | flops 268435456 | bytes 8388608 | tf_op jit(solution)/shard_map/pallas_call | solution.py:326
  92.7 0.9 copy.15
  93.6 0.7 copy.16
  94.3 1.3 %copy.27 = f32[8,128]{1,0:T(8,128)} copy(f32[8,128]{1,0:T(8,128)} %get-tuple-element.17) | data formatting | bytes 8192
  (2 shorter events, 0.0 us)
